TPU v7x, 32 devices: a whole 2x2x4 slice. The times are simulated.
32 devices in a mesh: groups: 2 (over y), rows: 8 (over z, x), cols: 2 (over core).
Axes of the slice: x: 2, y: 2, z: 4, core: 2. Of those that a mesh axis runs over, the one named last changes fastest.
Arguments:
- plume_field: bfloat16 [64, 64, 1024], P(None, ('groups', 'rows'), 'cols'), parts along dimension 1, may hold values from -6 to 6
- spectral_weight: bfloat16 [2, 1024, 64, 128], P(None, ('rows', 'cols')), may hold values from -0.5 to 0.5
- point_weight: bfloat16 [2, 64, 64], replicated, may hold values from -0.75 to 0.75
- conv_weight: bfloat16 [2, 3, 64, 64, 3, 3], replicated, may hold values from -0.25 to 0.25
Outputs:
- layer_output: bfloat16 [64, 64, 1024], P(None, ('groups', 'rows'), 'cols'), parts along dimension 1
There are 2 independent parts, one for each index of `groups`. A program takes and returns all parts, laid end to end along the dimension named above; an argument that names none is the same for every part. Nothing has to cross between parts.
All inputs are finite; a program needn't handle non-finite values.
Results may differ from a plain program's by a relative error of at most 0.015.
Values may be sent and summed in bfloat16 or wider, within the bound.
A program may use at most 64 MiB of HBM per device.

v0:
```python
import math

import functools

import jax
import jax.numpy as jnp
import numpy as np
from jax import lax
from jax.experimental import pallas as pl
from jax.experimental.pallas import tpu as pltpu
from jax.sharding import PartitionSpec as P

CH = 64
MR = 32
MC = 32
LAYERS = 2


def with_halo(cells, sides, width):
    for axis, dim in sides:
        count = lax.axis_size(axis)
        ends = count - 1
        head = lax.slice_in_dim(cells, 0, width, axis=dim)
        tail = lax.slice_in_dim(cells, cells.shape[dim] - width, cells.shape[dim], axis=dim)
        cells = jnp.concatenate(
            [
                lax.ppermute(tail, axis, [(i, (i + 1) % count) for i in range(ends)]),
                cells,
                lax.ppermute(head, axis, [((i + 1) % count, i) for i in range(ends)]),
            ],
            axis=dim,
        )
    return cells


def angles(frequencies, positions, extent):
    product = frequencies[:, None] * positions[None, :] % extent
    return 2.0 * math.pi / extent * product.astype(jnp.float32)


def row_frequencies(extent):
    wave_index = jnp.arange(MR, dtype=jnp.int32)
    return jnp.where(wave_index < MR // 2, wave_index, extent - MR + wave_index)


def contract(form, left, right):
    return jnp.einsum(form, left, right, precision=lax.Precision.HIGHEST)


def convolve_valid(padded, kernel):
    result = lax.conv_general_dilated(
        padded[None],
        kernel,
        (1, 1),
        "VALID",
        dimension_numbers=("NCHW", "OIHW", "NCHW"),
        preferred_element_type=jnp.float32,
    )
    return result[0]


def rim_once(values):
    return with_halo(values, (("rows", 1), ("cols", 2)), 1)


def shards(plume_field, spectral_weight, point_weight, conv_weight):
    rows_here, cols_here = (plume_field.shape[1], plume_field.shape[2])
    row_devices, col_devices = (lax.axis_size("rows"), lax.axis_size("cols"))
    row_count, col_count = (rows_here * row_devices, cols_here * col_devices)
    row_start = lax.axis_index("rows") * rows_here
    col_start = lax.axis_index("cols") * cols_here
    row_positions = row_start + jnp.arange(rows_here, dtype=jnp.int32)
    col_positions = col_start + jnp.arange(cols_here, dtype=jnp.int32)
    row_theta = angles(row_frequencies(row_count), row_positions, row_count)
    col_theta = angles(jnp.arange(MC, dtype=jnp.int32), col_positions, col_count)
    cos_rows, sin_rows = (jnp.cos(row_theta), jnp.sin(row_theta))
    all_theta = angles(
        row_frequencies(row_count), jnp.arange(row_count, dtype=jnp.int32), row_count
    )
    cos_every, sin_every = (jnp.cos(all_theta), jnp.sin(all_theta))
    forward_table = jnp.concatenate([jnp.cos(col_theta), jnp.sin(col_theta)], 0).T.astype(
        jnp.bfloat16
    )
    back_table = jnp.concatenate([jnp.cos(col_theta), -jnp.sin(col_theta)], 0)
    norm_factor = 1.0 / math.sqrt(row_count * col_count)
    owned_count = MR * MC // (row_devices * col_devices)
    block_count = MR * MC // row_devices
    block_width = min(block_count, MC)
    block_depth = max(block_count // MC, 1)
    spread = MC // block_width
    pairs_here = block_width * CH // row_devices
    for layer_index in range(LAYERS):
        partial_value = jnp.einsum(
            "cxy,yk->cxk", plume_field, forward_table, preferred_element_type=jnp.float32
        )
        banded = lax.psum(partial_value.astype(jnp.bfloat16), "cols").astype(jnp.float32)
        pencil = banded.reshape(CH, rows_here, 2, spread, block_width).transpose(4, 0, 2, 3, 1)
        pencil = pencil.reshape(block_width * CH, 2, spread, rows_here)
        columns = lax.all_to_all(
            pencil.astype(jnp.bfloat16), "rows", split_axis=0, concat_axis=3, tiled=True
        ).astype(pencil.dtype)
        part_re, part_im = (columns[:, 0], -columns[:, 1])
        four_re = contract("kx,qvx->qvk", cos_every, part_re) + contract(
            "kx,qvx->qvk", sin_every, part_im
        )
        four_im = contract("kx,qvx->qvk", cos_every, part_im) - contract(
            "kx,qvx->qvk", sin_every, part_re
        )
        pencil_spec = jnp.stack([four_re, four_im], 1) * norm_factor
        outgoing = pencil_spec.reshape(
            pairs_here, 2, spread, MR // block_depth, block_depth
        ).transpose(3, 2, 0, 1, 4)
        outgoing = outgoing.reshape(row_devices, pairs_here, 2, block_depth)
        arrived = lax.all_to_all(outgoing, "rows", split_axis=0, concat_axis=0, tiled=True)
        block_spec = (
            arrived.reshape(block_width, CH, 2, block_depth)
            .transpose(3, 0, 2, 1)
            .reshape(block_count, 2 * CH)
        )
        owned_spectrum = lax.dynamic_slice_in_dim(
            block_spec, lax.axis_index("cols") * owned_count, owned_count, 0
        )
        rounded = owned_spectrum.astype(jnp.bfloat16).astype(jnp.float32)
        weight_wide = spectral_weight[layer_index].astype(jnp.float32)
        from_re = contract("mc,mcd->md", rounded[:, :CH], weight_wide)
        from_im = contract("mc,mcd->md", rounded[:, CH:], weight_wide)
        owned_mixed = jnp.concatenate(
            [from_re[:, :CH] - from_im[:, CH:], from_re[:, CH:] + from_im[:, :CH]], -1
        ).astype(jnp.bfloat16)
        every_mode = lax.all_gather(owned_mixed, ("rows", "cols"), axis=0, tiled=True)
        every_mode = every_mode.astype(jnp.float32).reshape(MR, MC, 2 * CH)
        mode_re, mode_im = (every_mode[..., :CH], every_mode[..., CH:])
        back_re = contract("kx,kjc->jxc", cos_rows, mode_re) - contract(
            "kx,kjc->jxc", sin_rows, mode_im
        )
        back_im = contract("kx,kjc->jxc", sin_rows, mode_re) + contract(
            "kx,kjc->jxc", cos_rows, mode_im
        )
        stacked = jnp.concatenate([back_re, back_im], 0)
        spectral_part = contract("jxc,jy->cxy", stacked, back_table) / math.sqrt(MR * MC)
        point_part = jnp.einsum(
            "co,cxy->oxy",
            point_weight[layer_index],
            plume_field,
            preferred_element_type=jnp.float32,
        )
        kernels = conv_weight[layer_index]
        first = jax.nn.gelu(convolve_valid(rim_once(plume_field), kernels[0])).astype(jnp.bfloat16)
        second = jax.nn.gelu(convolve_valid(rim_once(first), kernels[1])).astype(jnp.bfloat16)
        branch_out = convolve_valid(rim_once(second), kernels[2])
        plume_field = jax.nn.gelu(spectral_part + point_part + branch_out).astype(jnp.bfloat16)
    return plume_field


HALO = 3
PAD = 128


def gelu(z):
    return 0.5 * z * (1.0 + jnp.tanh(math.sqrt(2.0 / math.pi) * (z + 0.044715 * z * z * z)))


def dot(a, b):
    return jnp.dot(a, b, preferred_element_type=jnp.float32)


def tables(row_count, col_count, col_devices):
    k = np.arange(MR)
    f1 = np.where(k < MR // 2, k, row_count - MR + k)
    row = 2.0 * math.pi / row_count * (f1[:, None] * np.arange(row_count)[None] % row_count)
    col = 2.0 * math.pi / col_count * (np.arange(MC)[:, None] * np.arange(col_count)[None] % col_count)
    split = lambda t: t.reshape(2 * MC, col_devices, -1).transpose(1, 0, 2)
    fwd = split(np.concatenate([np.cos(col), np.sin(col)], 0)).astype(jnp.bfloat16)
    back = split(np.concatenate([np.cos(col), -np.sin(col)], 0) / math.sqrt(MR * MC)).astype(jnp.bfloat16)
    return np.cos(row).astype(np.float32), np.sin(row).astype(np.float32), fwd, back


def fused(
    rd, x_ref, sw_ref, pw_ref, cw_ref, cos_ref, sin_ref, fwd_ref, back_ref, out_ref,
    v, kmat, x1, x2, rb, bsend, brecv, asend, arecv, gat, spec_out,
    h_send, h_recv, c_send, c_recv, a_send, a_recv, g_send, g_recv, f_send, f_recv,
):
    f32, bf16 = jnp.float32, jnp.bfloat16
    rows_here, _, cols_here = x_ref.shape
    wide = cols_here + PAD
    total_rows = rows_here + 2 * HALO
    owned = sw_ref.shape[1] // CH
    per_dest = owned // MC
    row_count = rows_here * rd
    norm = 1.0 / math.sqrt(row_count * cols_here * 2)
    r = lax.axis_index("rows")
    c = lax.axis_index("cols")
    sib = 1 - c
    row_at = lambda o: lax.rem(r + o + rd, rd)
    up, down = row_at(-1), row_at(1)

    def to(row, col):
        return {"rows": row, "cols": col}

    def remote(src, dst, ss, rs, row, col):
        return pltpu.make_async_remote_copy(
            src_ref=src, dst_ref=dst, send_sem=ss, recv_sem=rs,
            device_id=to(row, col), device_id_type=pl.DeviceIdType.MESH,
        )

    barrier = pltpu.get_barrier_semaphore()
    peers = [(row_at(o), c) for o in range(1, rd)] + [(r, sib), (up, sib), (down, sib)]
    for row, col in peers:
        pl.semaphore_signal(
            barrier, inc=1, device_id=to(row, col), device_id_type=pl.DeviceIdType.MESH
        )
    v[0, HALO:HALO + rows_here, :, 0:cols_here] = x_ref[...]
    pl.semaphore_wait(barrier, len(peers))

    edge = pl.multiple_of(sib * (cols_here - PAD), PAD)

    def halo_copies(l):
        vl = v.at[l]
        top, bottom = pl.ds(HALO, HALO), pl.ds(rows_here, HALO)
        own = pl.ds(HALO, rows_here)
        first_rows, last_rows = pl.ds(0, HALO), pl.ds(HALO + rows_here, HALO)
        body, rim, src_rim = pl.ds(0, cols_here), pl.ds(cols_here, PAD), pl.ds(edge, PAD)
        every = pl.ds(0, CH)
        plan = [
            (own, src_rim, own, rim, r, sib),
            (top, body, last_rows, body, up, c),
            (bottom, body, first_rows, body, down, c),
            (top, src_rim, last_rows, rim, up, sib),
            (bottom, src_rim, first_rows, rim, down, sib),
        ]
        return [
            remote(vl.at[sr, every, sc], vl.at[dr, every, dc], h_send.at[l, n], h_recv.at[l, n], row, col)
            for n, (sr, sc, dr, dc, row, col) in enumerate(plan)
        ]

    lane = lax.broadcasted_iota(jnp.int32, (1, wide), 1)
    mid = cols_here + PAD // 2
    low_side = (lane < mid).astype(f32)
    high_side = ((lane < cols_here) | (lane >= mid)).astype(f32)
    cf = c.astype(f32)
    lane_mask = low_side * (1.0 - cf) + high_side * cf
    sign = jnp.where(lax.broadcasted_iota(jnp.int32, (1, 2 * CH), 1) < CH, -1.0, 1.0).astype(f32)

    def mask_of(t):
        row = r * rows_here + t - HALO
        inside = jnp.where((row >= 0) & (row < row_count), 1.0, 0.0).astype(f32)
        return lane_mask * inside

    def stack(value):
        return jnp.concatenate(
            [pltpu.roll(value, 1, 1), value, pltpu.roll(value, wide - 1, 1)], 0
        ).astype(bf16)

    def build_weights(l):
        point = pw_ref[l].astype(f32).T
        none = jnp.zeros((CH, CH), f32)
        for s in range(3):
            for i in range(3):
                parts = [cw_ref[l, s, i, j].astype(f32) for j in range(3)]
                parts.append(point if (s == 2 and i == 1) else none)
                kmat[s, i * CH:(i + 1) * CH, :] = jnp.concatenate(parts, 1).astype(bf16)

    def summed(t):
        return rb[t - 1, 0:CH] + rb[t, CH:2 * CH] + rb[t + 1, 2 * CH:3 * CH]

    def conv_first(l):
        def one(t, carry):
            value = v[l, t].astype(f32) * mask_of(t)
            rb[t] = dot(kmat[0, :, 0:3 * CH], stack(value))
            return carry
        lax.fori_loop(0, total_rows, one, 0)
        def fin(t, carry):
            x1[t] = stack(gelu(summed(t)) * mask_of(t))
            return carry
        lax.fori_loop(1, total_rows - 1, fin, 0)

    def conv_second(l):
        def one(t, carry):
            rb[t] = dot(kmat[1, :, 0:3 * CH], x1[t])
            return carry
        lax.fori_loop(1, total_rows - 1, one, 0)
        def fin(t, carry):
            x2[t, 0:3 * CH] = stack(gelu(summed(t)) * mask_of(t))
            x2[t, 3 * CH:4 * CH] = v[l, t]
            return carry
        lax.fori_loop(2, total_rows - 2, fin, 0)

    def conv_third():
        def one(t, carry):
            rb[t] = dot(kmat[2], x2[t])
            return carry
        lax.fori_loop(2, total_rows - 2, one, 0)

    def row_block(us, ws, dest):
        parts = []
        for q in range(per_dest):
            k1 = (dest * 2 + c) * per_dest + q
            total = None
            for x in range(rows_here):
                at = r * rows_here + x
                term = cos_ref[k1, at] * us[x] + sin_ref[k1, at] * ws[x]
                total = term if total is None else total + term
            parts.append(total)
        return jnp.concatenate(parts, 0) if per_dest > 1 else parts[0]

    for l in range(LAYERS):
        halos = halo_copies(l)
        flat = v[l, HALO:HALO + rows_here, :, 0:cols_here].reshape(rows_here * CH, cols_here)
        bpart = lax.dot_general(
            fwd_ref[c], flat, (((1,), (1,)), ((), ())), preferred_element_type=f32
        )
        bsend[l] = bpart.astype(bf16)
        col_copy = remote(bsend.at[l], brecv.at[l], c_send.at[l], c_recv.at[l], r, sib)
        col_copy.start()
        for h in halos:
            h.start()
        build_weights(l)
        col_copy.wait_recv()
        cols_sum = bpart + brecv[l].astype(f32)
        us, ws = [], []
        for x in range(rows_here):
            re = cols_sum[0:MC, x * CH:(x + 1) * CH]
            im = -cols_sum[MC:2 * MC, x * CH:(x + 1) * CH]
            us.append(jnp.concatenate([re, im], 1))
            ws.append(jnp.concatenate([im, -re], 1))
        a_copies = []
        for o in range(1, rd):
            dest = row_at(o)
            asend[l, o] = row_block(us, ws, dest).astype(bf16)
            cp = remote(asend.at[l, o], arecv.at[l, o], a_send.at[l, o], a_recv.at[l, o], dest, c)
            cp.start()
            a_copies.append(cp)
        own_spec = row_block(us, ws, r)
        for h in halos:
            h.wait_recv()
        conv_first(l)
        for cp in a_copies:
            cp.wait_recv()
        spec = own_spec
        for o in range(1, rd):
            spec = spec + arecv[l, o].astype(f32)
        spec = spec * norm
        turned = pltpu.roll(spec, CH, 1)
        is_re = lax.broadcasted_iota(jnp.int32, (owned, 2 * CH), 1) < CH
        both = jnp.concatenate([jnp.where(is_re, spec, turned), jnp.where(is_re, turned, spec)], 0)
        mode_of_row = lax.rem(lax.broadcasted_iota(jnp.int32, (2 * owned, 2 * CH), 0), owned)
        half = lax.broadcasted_iota(jnp.int32, (2 * owned, 2 * CH), 1) // CH
        blocks = [
            jnp.where(mode_of_row == 2 * t + half, both, 0.0).astype(bf16) for t in range(owned // 2)
        ]
        mixed = dot(jnp.concatenate(blocks, 1), sw_ref[l])
        mixed = mixed[0:owned] + sign * pltpu.roll(mixed[owned:2 * owned], CH, 1)
        me = r * 2 + c
        gat[l, me] = mixed.astype(bf16)
        g_copies = []
        for o in range(1, rd):
            cp = remote(gat.at[l, me], gat.at[l, me], g_send.at[l, o], g_recv.at[l, o], row_at(o), c)
            cp.start()
            g_copies.append(cp)
        f_copies = [remote(gat.at[l, me], gat.at[l, me], f_send.at[l, 0], f_recv.at[l, 0], r, sib)]
        f_copies[0].start()
        conv_second(l)
        for o in range(1, rd):
            src = row_at(-o) * 2 + c
            remote(gat.at[l, src], gat.at[l, src], g_send.at[l, o], g_recv.at[l, o], row_at(o), c).wait_recv()
            cp = remote(gat.at[l, src], gat.at[l, src], f_send.at[l, o], f_recv.at[l, o], r, sib)
            cp.start()
            f_copies.append(cp)
        conv_third()

        sums = [None] * (2 * rows_here)

        def absorb(device):
            for q in range(per_dest):
                k1 = device * per_dest + q
                g = gat[l, device, q * MC:(q + 1) * MC].astype(f32)
                for x in range(rows_here):
                    at = r * rows_here + x
                    for n, tab in ((x, cos_ref), (rows_here + x, sin_ref)):
                        term = tab[k1, at] * g
                        sums[n] = term if sums[n] is None else sums[n] + term

        for o in range(rd):
            absorb(row_at(-o) * 2 + c)
        for o in range(rd):
            src = row_at(-o) * 2 + sib
            remote(gat.at[l, src], gat.at[l, src], f_send.at[l, o], f_recv.at[l, o], r, sib).wait_recv()
            absorb(src)
        backs = [sums[x] + sign * pltpu.roll(sums[rows_here + x], CH, 1) for x in range(rows_here)]
        backs = jnp.concatenate(
            [
                jnp.concatenate([b[:, 0:CH] for b in backs], 1),
                jnp.concatenate([b[:, CH:2 * CH] for b in backs], 1),
            ],
            0,
        )
        spec_out[...] = dot(backs.T.astype(bf16), back_ref[c])
        for x in range(rows_here):
            t = HALO + x
            result = gelu(
                spec_out[x * CH:(x + 1) * CH]
                + rb[t - 1, 0:CH, 0:cols_here]
                + rb[t, CH:2 * CH, 0:cols_here]
                + rb[t + 1, 2 * CH:3 * CH, 0:cols_here]
            ).astype(bf16)
            if l + 1 < LAYERS:
                v[l + 1, t, :, 0:cols_here] = result
            else:
                out_ref[x] = result
        for cp in [col_copy] + halos + a_copies + g_copies + f_copies:
            cp.wait_send()


def fused_shards(plume_field, spectral_weight, point_weight, conv_weight):
    _, rows_here, cols_here = plume_field.shape
    rd, cd = lax.axis_size("rows"), lax.axis_size("cols")
    owned = spectral_weight.shape[1]
    cos_t, sin_t, fwd, back = tables(rows_here * rd, cols_here * cd, cd)
    wide, total_rows = cols_here + PAD, rows_here + 2 * HALO
    f32, bf16 = jnp.float32, jnp.bfloat16
    vm = pl.BlockSpec(memory_space=pltpu.VMEM)
    sm = pl.BlockSpec(memory_space=pltpu.SMEM)
    dma = pltpu.SemaphoreType.DMA
    out = pl.pallas_call(
        functools.partial(fused, rd),
        out_shape=jax.ShapeDtypeStruct((rows_here, CH, cols_here), bf16),
        in_specs=[vm, vm, vm, vm, sm, sm, vm, vm],
        out_specs=vm,
        scratch_shapes=[
            pltpu.VMEM((LAYERS, total_rows, CH, wide), bf16),
            pltpu.VMEM((3, 3 * CH, 4 * CH), bf16),
            pltpu.VMEM((total_rows, 3 * CH, wide), bf16),
            pltpu.VMEM((total_rows, 4 * CH, wide), bf16),
            pltpu.VMEM((total_rows, 3 * CH, wide), f32),
            pltpu.VMEM((LAYERS, 2 * MC, rows_here * CH), bf16),
            pltpu.VMEM((LAYERS, 2 * MC, rows_here * CH), bf16),
            pltpu.VMEM((LAYERS, rd, owned, 2 * CH), bf16),
            pltpu.VMEM((LAYERS, rd, owned, 2 * CH), bf16),
            pltpu.VMEM((LAYERS, rd * cd, owned, 2 * CH), bf16),
            pltpu.VMEM((rows_here * CH, cols_here), f32),
            dma((LAYERS, 5)), dma((LAYERS, 5)),
            dma((LAYERS,)), dma((LAYERS,)),
            dma((LAYERS, rd)), dma((LAYERS, rd)),
            dma((LAYERS, rd)), dma((LAYERS, rd)),
            dma((LAYERS, rd)), dma((LAYERS, rd)),
        ],
        compiler_params=pltpu.CompilerParams(
            collective_id=0, has_side_effects=True, vmem_limit_bytes=48 * 1024 * 1024
        ),
    )(
        plume_field.transpose(1, 0, 2),
        spectral_weight.reshape(LAYERS, owned * CH, 2 * CH),
        point_weight,
        conv_weight.transpose(0, 1, 4, 5, 2, 3),
        cos_t, sin_t, fwd, back,
    )
    return out.transpose(1, 0, 2)


def routed(plume_field, spectral_weight, point_weight, conv_weight):
    _, rows_here, cols_here = plume_field.shape
    rd, cd = lax.axis_size("rows"), lax.axis_size("cols")
    owned = spectral_weight.shape[1]
    fits = (
        cd == 2 and 4 <= rd <= 16 and HALO <= rows_here <= 8
        and cols_here % PAD == 0 and cols_here <= 1024 and owned % MC == 0
    )
    return (fused_shards if fits else shards)(plume_field, spectral_weight, point_weight, conv_weight)


def solution(mesh):
    in_specs = (
        P(None, ("groups", "rows"), "cols"),
        P(None, ("rows", "cols"), None, None),
        P(),
        P(),
    )
    out_specs = P(None, ("groups", "rows"), "cols")
    return jax.shard_map(routed, mesh=mesh, in_specs=in_specs, out_specs=out_specs, check_vma=False)
```

profile of v0, /device:TPU:0, one launch (start us, length us, event | category | flops | bytes accessed | tf_op | source)
XLA Modules:
  0.0 67.3 jit_solution(11151280131529311108)
XLA Ops:
  0.0 1.0 %copy.12 = bf16[64,4,512]{2,0,1:T(8,128)(2,1)S(1)} copy(bf16[64,4,512]{2,1,0:T(4,128)(2,1)} %param.8) | data formatting | bytes 524288 | tf_op args[0]
  1.0 0.0 copy-start
  1.0 1.6 %copy-done = bf16[2,64,64,128]{3,2,1,0:T(8,128)(2,1)S(1)} copy-done((bf16[2,64,64,128]{3,2,1,0:T(8,128)(2,1)S(1)}, bf16[2,64,64,128]{3,2,1,0:T(8,128)(2,1)}, u32[]{:S(2)}) %copy-start) | copy-done | bytes 2097176
  2.6 0.0 copy-start.1
  2.6 1.2 %copy-done.1 = bf16[2,3,64,64,3,3]{3,2,5,4,1,0:T(8,128)(2,1)S(1)} copy-done((bf16[2,3,64,64,3,3]{3,2,5,4,1,0:T(8,128)(2,1)S(1)}, bf16[2,3,64,64,3,3]{3,2,5,4,1,0:T(8,128)(2,1)}, u32[]{:S(2)}) %copy-start.1) | copy-done | bytes 442392
  3.8 0.0 copy-start.2
  3.8 0.9 %copy-done.2 = bf16[2,64,512]{2,1,0:T(8,128)(2,1)S(1)} copy-done((bf16[2,64,512]{2,1,0:T(8,128)(2,1)S(1)}, bf16[2,64,512]{2,1,0:T(8,128)(2,1)}, u32[]{:S(2)}) %copy-start.2) | copy-done | bytes 131096
  4.7 0.0 copy-start.3
  4.7 0.9 %copy-done.3 = bf16[2,64,512]{2,1,0:T(8,128)(2,1)S(1)} copy-done((bf16[2,64,512]{2,1,0:T(8,128)(2,1)S(1)}, bf16[2,64,512]{2,1,0:T(8,128)(2,1)}, u32[]{:S(2)}) %copy-start.3) | copy-done | bytes 131096
  5.6 0.0 copy-start.4
  5.6 0.8 %copy-done.4 = bf16[2,64,64]{2,1,0:T(8,128)(2,1)S(1)} copy-done((bf16[2,64,64]{2,1,0:T(8,128)(2,1)S(1)}, bf16[2,64,64]{2,1,0:T(8,128)(2,1)}, u32[]{:S(2)}) %copy-start.4) | copy-done | bytes 16408
  6.3 0.0 copy-start.5
  6.3 0.7 %copy-done.5 = f32[32,32]{1,0:T(8,128)S(1)} copy-done((f32[32,32]{1,0:T(8,128)S(1)}, f32[32,32]{1,0:T(8,128)}, u32[]{:S(2)}) %copy-start.5) | copy-done | bytes 4120
  7.0 0.0 copy-start.6
  7.0 0.7 %copy-done.6 = f32[32,32]{1,0:T(8,128)S(1)} copy-done((f32[32,32]{1,0:T(8,128)S(1)}, f32[32,32]{1,0:T(8,128)}, u32[]{:S(2)}) %copy-start.6) | copy-done | bytes 4120
  7.8 58.7 %shard_map.82 = bf16[4,64,512]{2,1,0:T(8,128)(2,1)S(1)} custom-call(bf16[4,64,512]{2,1,0:T(8,128)(2,1)S(1)} %bitcast.8, bf16[2,4096,128]{2,1,0:T(8,128)(2,1)S(1)} %bitcast.6, bf16[2,64,64]{2,1,0:T(8,128)(2,1)S(1)} %copy-done.4, bf16[2,3,3,3,64,64]{5,4,3,2,1,0:T(8,128)(2,1)S(1)} %bitcast.9, f32[32,32]{1,0:T(8,128)S(1)} %copy-done.6, f32[32,32]{1,0:T(8,128)S(1)} %copy-done.5, ...), custom_call_target="tpu_custom_call" | custom-call | tf_op jit(solution)/shard_map/pallas_call | solution.py:424
  66.4 0.9 %copy.10 = bf16[64,4,512]{2,1,0:T(4,128)(2,1)} copy(bf16[64,4,512]{2,0,1:T(8,128)(2,1)S(1)} %bitcast.7) | data formatting | bytes 524288 | tf_op jit(solution)/shard_map/transpose | solution.py:457
Async XLA Ops:
  1.0 1.6 %copy-start = (bf16[2,64,64,128]{3,2,1,0:T(8,128)(2,1)S(1)}, bf16[2,64,64,128]{3,2,1,0:T(8,128)(2,1)}, u32[]{:S(2)}) copy-start(bf16[2,64,64,128]{3,2,1,0:T(8,128)(2,1)} %param.9) | copy-start | bytes 6291460
  2.6 1.2 %copy-start.1 = (bf16[2,3,64,64,3,3]{3,2,5,4,1,0:T(8,128)(2,1)S(1)}, bf16[2,3,64,64,3,3]{3,2,5,4,1,0:T(8,128)(2,1)}, u32[]{:S(2)}) copy-start(bf16[2,3,64,64,3,3]{3,2,5,4,1,0:T(8,128)(2,1)} %param.11) | copy-start | bytes 1327108
  3.8 0.9 %copy-start.2 = (bf16[2,64,512]{2,1,0:T(8,128)(2,1)S(1)}, bf16[2,64,512]{2,1,0:T(8,128)(2,1)}, u32[]{:S(2)}) copy-start(bf16[2,64,512]{2,1,0:T(8,128)(2,1)} %constant.11.clone.back_ref) | copy-start | bytes 393220
  4.7 0.9 %copy-start.3 = (bf16[2,64,512]{2,1,0:T(8,128)(2,1)S(1)}, bf16[2,64,512]{2,1,0:T(8,128)(2,1)}, u32[]{:S(2)}) copy-start(bf16[2,64,512]{2,1,0:T(8,128)(2,1)} %constant.10.clone.fwd_ref) | copy-start | bytes 393220
  5.6 0.8 %copy-start.4 = (bf16[2,64,64]{2,1,0:T(8,128)(2,1)S(1)}, bf16[2,64,64]{2,1,0:T(8,128)(2,1)}, u32[]{:S(2)}) copy-start(bf16[2,64,64]{2,1,0:T(8,128)(2,1)} %pw_ref.1) | copy-start | bytes 49156
  6.3 0.7 %copy-start.5 = (f32[32,32]{1,0:T(8,128)S(1)}, f32[32,32]{1,0:T(8,128)}, u32[]{:S(2)}) copy-start(f32[32,32]{1,0:T(8,128)} %constant.9.clone.sin_ref) | copy-start | bytes 12292
  7.0 0.7 %copy-start.6 = (f32[32,32]{1,0:T(8,128)S(1)}, f32[32,32]{1,0:T(8,128)}, u32[]{:S(2)}) copy-start(f32[32,32]{1,0:T(8,128)} %constant.8.clone.cos_ref) | copy-start | bytes 12292
where the time goes:
time: 67.8 us; the launch traced here: 67.3 us
  Pallas kernels  58.7 us (87%)
  local copies, waits for them, and re-layouts  8.65 us (13%)
    pallas_call x1, Pallas kernels, fused_shards(): pl.pallas_call(functools.partial(fused, rd), out_shape=jax.ShapeDtypeStru...  58.7 us
    unnamed x15, local copies, waits for them, and re-layouts  7.75 us

commit v1 on v0

--- a/solution.py
+++ b/solution.py
@@ -153,6 +153,7 @@
 
 
 HALO = 3
+EARLY = False
 PAD = 128
 
 
@@ -172,11 +173,14 @@
     split = lambda t: t.reshape(2 * MC, col_devices, -1).transpose(1, 0, 2)
     fwd = split(np.concatenate([np.cos(col), np.sin(col)], 0)).astype(jnp.bfloat16)
     back = split(np.concatenate([np.cos(col), -np.sin(col)], 0) / math.sqrt(MR * MC)).astype(jnp.bfloat16)
-    return np.cos(row).astype(np.float32), np.sin(row).astype(np.float32), fwd, back
+    trig = np.concatenate([np.cos(row), np.sin(row)], 0).astype(np.float32)
+    trig = np.pad(trig, ((0, 0), (0, -row_count % PAD)))
+    return trig, fwd, back
 
 
 def fused(
-    rd, x_ref, sw_ref, pw_ref, cw_ref, cos_ref, sin_ref, fwd_ref, back_ref, out_ref,
+    rd, x_ref, sw_hbm, pw_hbm, cw_hbm, trig_hbm, fwd_hbm, back_hbm, out_ref,
+    sw_ref, pw_ref, cw_ref, trig, fwd_ref, back_ref, l_sem,
     v, kmat, x1, x2, rb, bsend, brecv, asend, arecv, gat, spec_out,
     h_send, h_recv, c_send, c_recv, a_send, a_recv, g_send, g_recv, f_send, f_recv,
 ):
@@ -184,7 +188,7 @@
     rows_here, _, cols_here = x_ref.shape
     wide = cols_here + PAD
     total_rows = rows_here + 2 * HALO
-    owned = sw_ref.shape[1] // CH
+    owned = sw_hbm.shape[1] // CH
     per_dest = owned // MC
     row_count = rows_here * rd
     norm = 1.0 / math.sqrt(row_count * cols_here * 2)
@@ -204,13 +208,31 @@
         )
 
     barrier = pltpu.get_barrier_semaphore()
-    peers = [(row_at(o), c) for o in range(1, rd)] + [(r, sib), (up, sib), (down, sib)]
+    peers = [(row_at(o), c) for o in range(1, rd)] + [(r, sib)]
     for row, col in peers:
         pl.semaphore_signal(
             barrier, inc=1, device_id=to(row, col), device_id_type=pl.DeviceIdType.MESH
         )
+    loads = [
+        pltpu.make_async_copy(src, dst, l_sem.at[n])
+        for n, (src, dst) in enumerate(
+            (
+                (fwd_hbm.at[c], fwd_ref), (cw_hbm, cw_ref), (pw_hbm, pw_ref),
+                (trig_hbm, trig), (sw_hbm, sw_ref), (back_hbm.at[c], back_ref),
+            )
+        )
+    ]
+    for load in loads:
+        load.start()
     v[0, HALO:HALO + rows_here, :, 0:cols_here] = x_ref[...]
-    pl.semaphore_wait(barrier, len(peers))
+
+    @pl.when(r == 0)
+    def _():
+        v[:, 0:HALO, :, 0:cols_here] = jnp.zeros((LAYERS, HALO, CH, cols_here), bf16)
+
+    @pl.when(r == rd - 1)
+    def _():
+        v[:, HALO + rows_here:, :, 0:cols_here] = jnp.zeros((LAYERS, HALO, CH, cols_here), bf16)
 
     edge = pl.multiple_of(sib * (cols_here - PAD), PAD)
 
@@ -222,16 +244,18 @@
         body, rim, src_rim = pl.ds(0, cols_here), pl.ds(cols_here, PAD), pl.ds(edge, PAD)
         every = pl.ds(0, CH)
         plan = [
-            (own, src_rim, own, rim, r, sib),
             (top, body, last_rows, body, up, c),
             (bottom, body, first_rows, body, down, c),
-            (top, src_rim, last_rows, rim, up, sib),
-            (bottom, src_rim, first_rows, rim, down, sib),
+            (own, src_rim, own, rim, r, sib),
+            (first_rows, src_rim, first_rows, rim, r, sib),
+            (last_rows, src_rim, last_rows, rim, r, sib),
         ]
         return [
             remote(vl.at[sr, every, sc], vl.at[dr, every, dc], h_send.at[l, n], h_recv.at[l, n], row, col)
             for n, (sr, sc, dr, dc, row, col) in enumerate(plan)
         ]
+
+    has_up, has_down = r > 0, r < rd - 1
 
     lane = lax.broadcasted_iota(jnp.int32, (1, wide), 1)
     mid = cols_here + PAD // 2
@@ -263,12 +287,14 @@
     def summed(t):
         return rb[t - 1, 0:CH] + rb[t, CH:2 * CH] + rb[t + 1, 2 * CH:3 * CH]
 
-    def conv_first(l):
+    def conv_rows(l, low, high):
         def one(t, carry):
             value = v[l, t].astype(f32) * mask_of(t)
             rb[t] = dot(kmat[0, :, 0:3 * CH], stack(value))
             return carry
-        lax.fori_loop(0, total_rows, one, 0)
+        lax.fori_loop(low, high, one, 0)
+
+    def conv_first():
         def fin(t, carry):
             x1[t] = stack(gelu(summed(t)) * mask_of(t))
             return carry
@@ -298,7 +324,7 @@
             total = None
             for x in range(rows_here):
                 at = r * rows_here + x
-                term = cos_ref[k1, at] * us[x] + sin_ref[k1, at] * ws[x]
+                term = trig[k1, at] * us[x] + trig[MR + k1, at] * ws[x]
                 total = term if total is None else total + term
             parts.append(total)
         return jnp.concatenate(parts, 0) if per_dest > 1 else parts[0]
@@ -306,14 +332,23 @@
     for l in range(LAYERS):
         halos = halo_copies(l)
         flat = v[l, HALO:HALO + rows_here, :, 0:cols_here].reshape(rows_here * CH, cols_here)
+        if l == 0:
+            loads[0].wait()
         bpart = lax.dot_general(
-            fwd_ref[c], flat, (((1,), (1,)), ((), ())), preferred_element_type=f32
+            fwd_ref[...], flat, (((1,), (1,)), ((), ())), preferred_element_type=f32
         )
         bsend[l] = bpart.astype(bf16)
         col_copy = remote(bsend.at[l], brecv.at[l], c_send.at[l], c_recv.at[l], r, sib)
+        if l == 0:
+            pl.semaphore_wait(barrier, len(peers))
         col_copy.start()
-        for h in halos:
-            h.start()
+        halos[2].start()
+        if EARLY:
+            pl.when(has_up)(halos[0].start)
+            pl.when(has_down)(halos[1].start)
+        if l == 0:
+            for load in loads[1:4]:
+                load.wait()
         build_weights(l)
         col_copy.wait_recv()
         cols_sum = bpart + brecv[l].astype(f32)
@@ -330,10 +365,15 @@
             cp = remote(asend.at[l, o], arecv.at[l, o], a_send.at[l, o], a_recv.at[l, o], dest, c)
             cp.start()
             a_copies.append(cp)
+        if not EARLY:
+            pl.when(has_up)(halos[0].start)
+            pl.when(has_down)(halos[1].start)
         own_spec = row_block(us, ws, r)
-        for h in halos:
-            h.wait_recv()
-        conv_first(l)
+        halos[2].wait_recv()
+        conv_rows(l, HALO, HALO + rows_here)
+        if l == 0:
+            for load in loads[4:]:
+                load.wait()
         for cp in a_copies:
             cp.wait_recv()
         spec = own_spec
@@ -359,13 +399,22 @@
             g_copies.append(cp)
         f_copies = [remote(gat.at[l, me], gat.at[l, me], f_send.at[l, 0], f_recv.at[l, 0], r, sib)]
         f_copies[0].start()
-        conv_second(l)
+        pl.when(has_up)(halos[1].wait_recv)
+        pl.when(has_down)(halos[0].wait_recv)
+        for h in halos[3:]:
+            h.start()
         for o in range(1, rd):
             src = row_at(-o) * 2 + c
             remote(gat.at[l, src], gat.at[l, src], g_send.at[l, o], g_recv.at[l, o], row_at(o), c).wait_recv()
             cp = remote(gat.at[l, src], gat.at[l, src], f_send.at[l, o], f_recv.at[l, o], r, sib)
             cp.start()
             f_copies.append(cp)
+        for h in halos[3:]:
+            h.wait_recv()
+        conv_rows(l, 0, HALO)
+        conv_rows(l, HALO + rows_here, total_rows)
+        conv_first()
+        conv_second(l)
         conv_third()
 
         sums = [None] * (2 * rows_here)
@@ -376,8 +425,8 @@
                 g = gat[l, device, q * MC:(q + 1) * MC].astype(f32)
                 for x in range(rows_here):
                     at = r * rows_here + x
-                    for n, tab in ((x, cos_ref), (rows_here + x, sin_ref)):
-                        term = tab[k1, at] * g
+                    for n, base in ((x, 0), (rows_here + x, MR)):
+                        term = trig[base + k1, at] * g
                         sums[n] = term if sums[n] is None else sums[n] + term
 
         for o in range(rd):
@@ -394,7 +443,7 @@
             ],
             0,
         )
-        spec_out[...] = dot(backs.T.astype(bf16), back_ref[c])
+        spec_out[...] = dot(backs.T.astype(bf16), back_ref[...])
         for x in range(rows_here):
             t = HALO + x
             result = gelu(
@@ -407,7 +456,9 @@
                 v[l + 1, t, :, 0:cols_here] = result
             else:
                 out_ref[x] = result
-        for cp in [col_copy] + halos + a_copies + g_copies + f_copies:
+        pl.when(has_up)(halos[0].wait_send)
+        pl.when(has_down)(halos[1].wait_send)
+        for cp in [col_copy] + halos[2:] + a_copies + g_copies + f_copies:
             cp.wait_send()
 
 
@@ -415,18 +466,25 @@
     _, rows_here, cols_here = plume_field.shape
     rd, cd = lax.axis_size("rows"), lax.axis_size("cols")
     owned = spectral_weight.shape[1]
-    cos_t, sin_t, fwd, back = tables(rows_here * rd, cols_here * cd, cd)
+    trig, fwd, back = tables(rows_here * rd, cols_here * cd, cd)
     wide, total_rows = cols_here + PAD, rows_here + 2 * HALO
     f32, bf16 = jnp.float32, jnp.bfloat16
     vm = pl.BlockSpec(memory_space=pltpu.VMEM)
-    sm = pl.BlockSpec(memory_space=pltpu.SMEM)
+    hbm = pl.BlockSpec(memory_space=pltpu.HBM)
     dma = pltpu.SemaphoreType.DMA
     out = pl.pallas_call(
         functools.partial(fused, rd),
         out_shape=jax.ShapeDtypeStruct((rows_here, CH, cols_here), bf16),
-        in_specs=[vm, vm, vm, vm, sm, sm, vm, vm],
+        in_specs=[vm] + [hbm] * 6,
         out_specs=vm,
         scratch_shapes=[
+            pltpu.VMEM((LAYERS, owned * CH, 2 * CH), bf16),
+            pltpu.VMEM(point_weight.shape, bf16),
+            pltpu.VMEM((LAYERS, 3, 3, 3, CH, CH), bf16),
+            pltpu.SMEM((2 * MR, PAD * (-(-rows_here * rd // PAD))), f32),
+            pltpu.VMEM((2 * MC, cols_here), bf16),
+            pltpu.VMEM((2 * MC, cols_here), bf16),
+            dma((6,)),
             pltpu.VMEM((LAYERS, total_rows, CH, wide), bf16),
             pltpu.VMEM((3, 3 * CH, 4 * CH), bf16),
             pltpu.VMEM((total_rows, 3 * CH, wide), bf16),
@@ -445,14 +503,14 @@
             dma((LAYERS, rd)), dma((LAYERS, rd)),
         ],
         compiler_params=pltpu.CompilerParams(
-            collective_id=0, has_side_effects=True, vmem_limit_bytes=48 * 1024 * 1024
+            collective_id=0, has_side_effects=True, vmem_limit_bytes=63 * 1024 * 1024
         ),
     )(
         plume_field.transpose(1, 0, 2),
         spectral_weight.reshape(LAYERS, owned * CH, 2 * CH),
         point_weight,
         conv_weight.transpose(0, 1, 4, 5, 2, 3),
-        cos_t, sin_t, fwd, back,
+        trig, fwd, back,
     )
     return out.transpose(1, 0, 2)
 

time: 67.8 us -> 58 us (0.86)
  the two profiles are of different devices: /device:TPU:0 before, /device:TPU:13 now
where the time goes in v1:
time: 58 us; the launch traced here: 57.8 us
  Pallas kernels  54.2 us (93%)
  local copies, waits for them, and re-layouts  3.55 us (6%)
    pallas_call x1, Pallas kernels, fused_shards(): pl.pallas_call(functools.partial(fused, rd), out_shape=jax.ShapeDtypeStru...  54.2 us
    transpose x1, local copies, waits for them, and re-layouts, fused_shards(): return out.transpose(1, 0, 2)  1.86 us
    unnamed x1, local copies, waits for them, and re-layouts  1.7 us

profile of v1, /device:TPU:13, one launch (start us, length us, event | category | flops | bytes accessed | tf_op | source)
XLA Modules:
  0.0 57.8 jit_solution(6756562528358951836)
XLA Ops:
  0.0 1.7 %copy.11 = bf16[64,4,512]{2,0,1:T(8,128)(2,1)} copy(bf16[64,4,512]{2,1,0:T(4,128)(2,1)} %param.7) | data formatting | bytes 524288 | tf_op args[0]
  1.7 54.2 %shard_map.73 = bf16[4,64,512]{2,1,0:T(8,128)(2,1)} custom-call(bf16[4,64,512]{2,1,0:T(8,128)(2,1)} %bitcast.8, bf16[2,4096,128]{2,1,0:T(8,128)(2,1)} %bitcast.6, bf16[2,64,64]{2,1,0:T(8,128)(2,1)} %pw_hbm.1, bf16[2,3,3,3,64,64]{5,4,3,2,1,0:T(8,128)(2,1)} %bitcast.9, f32[64,128]{1,0:T(8,128)} %constant.6.clone.trig_hbm, ...), custom_call_target="tpu_custom_call" | custom-call | tf_op jit(solution)/shard_map/pallas_call | solution.py:475
  56.0 1.9 %copy.9 = bf16[64,4,512]{2,1,0:T(4,128)(2,1)} copy(bf16[64,4,512]{2,0,1:T(8,128)(2,1)} %bitcast.7) | data formatting | bytes 524288 | tf_op jit(solution)/shard_map/transpose | solution.py:515

commit v2 on v1

--- a/solution.py
+++ b/solution.py
@@ -153,7 +153,7 @@
 
 
 HALO = 3
-EARLY = False
+UNROLL = 2
 PAD = 128
 
 
@@ -181,7 +181,7 @@
 def fused(
     rd, x_ref, sw_hbm, pw_hbm, cw_hbm, trig_hbm, fwd_hbm, back_hbm, out_ref,
     sw_ref, pw_ref, cw_ref, trig, fwd_ref, back_ref, l_sem,
-    v, kmat, x1, x2, rb, bsend, brecv, asend, arecv, gat, spec_out,
+    v, kmat, rb, rb2, bsend, brecv, asend, arecv, gat, spec_out,
     h_send, h_recv, c_send, c_recv, a_send, a_recv, g_send, g_recv, f_send, f_recv,
 ):
     f32, bf16 = jnp.float32, jnp.bfloat16
@@ -284,38 +284,29 @@
                 parts.append(point if (s == 2 and i == 1) else none)
                 kmat[s, i * CH:(i + 1) * CH, :] = jnp.concatenate(parts, 1).astype(bf16)
 
-    def summed(t):
-        return rb[t - 1, 0:CH] + rb[t, CH:2 * CH] + rb[t + 1, 2 * CH:3 * CH]
-
-    def conv_rows(l, low, high):
+    def summed(rows, t):
+        return rows[t - 1, 0:CH] + rows[t, CH:2 * CH] + rows[t + 1, 2 * CH:3 * CH]
+
+    def conv_first(l, low, high):
         def one(t, carry):
             value = v[l, t].astype(f32) * mask_of(t)
             rb[t] = dot(kmat[0, :, 0:3 * CH], stack(value))
             return carry
-        lax.fori_loop(low, high, one, 0)
-
-    def conv_first():
-        def fin(t, carry):
-            x1[t] = stack(gelu(summed(t)) * mask_of(t))
+        lax.fori_loop(low, high, one, 0, unroll=min(UNROLL, high - low))
+
+    def conv_second(low, high):
+        def one(t, carry):
+            value = gelu(summed(rb, t)) * mask_of(t)
+            rb2[t] = dot(kmat[1, :, 0:3 * CH], stack(value))
             return carry
-        lax.fori_loop(1, total_rows - 1, fin, 0)
-
-    def conv_second(l):
+        lax.fori_loop(low, high, one, 0, unroll=min(UNROLL, high - low))
+
+    def conv_third(l):
         def one(t, carry):
-            rb[t] = dot(kmat[1, :, 0:3 * CH], x1[t])
+            value = gelu(summed(rb2, t)) * mask_of(t)
+            rb[t] = dot(kmat[2], jnp.concatenate([stack(value), v[l, t]], 0))
             return carry
-        lax.fori_loop(1, total_rows - 1, one, 0)
-        def fin(t, carry):
-            x2[t, 0:3 * CH] = stack(gelu(summed(t)) * mask_of(t))
-            x2[t, 3 * CH:4 * CH] = v[l, t]
-            return carry
-        lax.fori_loop(2, total_rows - 2, fin, 0)
-
-    def conv_third():
-        def one(t, carry):
-            rb[t] = dot(kmat[2], x2[t])
-            return carry
-        lax.fori_loop(2, total_rows - 2, one, 0)
+        lax.fori_loop(2, total_rows - 2, one, 0, unroll=UNROLL)
 
     def row_block(us, ws, dest):
         parts = []
@@ -343,9 +334,6 @@
             pl.semaphore_wait(barrier, len(peers))
         col_copy.start()
         halos[2].start()
-        if EARLY:
-            pl.when(has_up)(halos[0].start)
-            pl.when(has_down)(halos[1].start)
         if l == 0:
             for load in loads[1:4]:
                 load.wait()
@@ -365,12 +353,12 @@
             cp = remote(asend.at[l, o], arecv.at[l, o], a_send.at[l, o], a_recv.at[l, o], dest, c)
             cp.start()
             a_copies.append(cp)
-        if not EARLY:
-            pl.when(has_up)(halos[0].start)
-            pl.when(has_down)(halos[1].start)
+        pl.when(has_up)(halos[0].start)
+        pl.when(has_down)(halos[1].start)
         own_spec = row_block(us, ws, r)
         halos[2].wait_recv()
-        conv_rows(l, HALO, HALO + rows_here)
+        conv_first(l, HALO, HALO + rows_here)
+        conv_second(HALO + 1, HALO + rows_here - 1)
         if l == 0:
             for load in loads[4:]:
                 load.wait()
@@ -403,19 +391,19 @@
         pl.when(has_down)(halos[0].wait_recv)
         for h in halos[3:]:
             h.start()
+        for h in halos[3:]:
+            h.wait_recv()
+        conv_first(l, 0, HALO)
+        conv_first(l, HALO + rows_here, total_rows)
+        conv_second(1, HALO + 1)
+        conv_second(HALO + rows_here - 1, total_rows - 1)
         for o in range(1, rd):
             src = row_at(-o) * 2 + c
             remote(gat.at[l, src], gat.at[l, src], g_send.at[l, o], g_recv.at[l, o], row_at(o), c).wait_recv()
             cp = remote(gat.at[l, src], gat.at[l, src], f_send.at[l, o], f_recv.at[l, o], r, sib)
             cp.start()
             f_copies.append(cp)
-        for h in halos[3:]:
-            h.wait_recv()
-        conv_rows(l, 0, HALO)
-        conv_rows(l, HALO + rows_here, total_rows)
-        conv_first()
-        conv_second(l)
-        conv_third()
+        conv_third(l)
 
         sums = [None] * (2 * rows_here)
 
@@ -487,8 +475,7 @@
             dma((6,)),
             pltpu.VMEM((LAYERS, total_rows, CH, wide), bf16),
             pltpu.VMEM((3, 3 * CH, 4 * CH), bf16),
-            pltpu.VMEM((total_rows, 3 * CH, wide), bf16),
-            pltpu.VMEM((total_rows, 4 * CH, wide), bf16),
+            pltpu.VMEM((total_rows, 3 * CH, wide), f32),
             pltpu.VMEM((total_rows, 3 * CH, wide), f32),
             pltpu.VMEM((LAYERS, 2 * MC, rows_here * CH), bf16),
             pltpu.VMEM((LAYERS, 2 * MC, rows_here * CH), bf16),

time: 58 us -> 48.6 us (0.84)
  Pallas kernels: 54.2 us -> 44.8 us
    pallas_call x1, Pallas kernels: 54.2 us -> 44.8 us  [fused_shards(): pl.pallas_call(functools.partial(fused, rd), out_shape=jax.ShapeDtypeStru...]
where the time goes in v2:
time: 48.6 us; the launch traced here: 48.4 us
  Pallas kernels  44.8 us (92%)
  local copies, waits for them, and re-layouts  3.55 us (7%)
    pallas_call x1, Pallas kernels, fused_shards(): pl.pallas_call(functools.partial(fused, rd), out_shape=jax.ShapeDtypeStru...  44.8 us
    transpose x1, local copies, waits for them, and re-layouts, fused_shards(): return out.transpose(1, 0, 2)  1.86 us
    unnamed x1, local copies, waits for them, and re-layouts  1.7 us

profile of v2, /device:TPU:13, one launch (start us, length us, event | category | flops | bytes accessed | tf_op | source)
XLA Modules:
  0.0 48.4 jit_solution(6219139807846938315)
XLA Ops:
  0.0 1.7 %copy.11 = bf16[64,4,512]{2,0,1:T(8,128)(2,1)} copy(bf16[64,4,512]{2,1,0:T(4,128)(2,1)} %param.7) | data formatting | bytes 524288 | tf_op args[0]
  1.7 44.8 %shard_map.73 = bf16[4,64,512]{2,1,0:T(8,128)(2,1)} custom-call(bf16[4,64,512]{2,1,0:T(8,128)(2,1)} %bitcast.8, bf16[2,4096,128]{2,1,0:T(8,128)(2,1)} %bitcast.6, bf16[2,64,64]{2,1,0:T(8,128)(2,1)} %pw_hbm.1, bf16[2,3,3,3,64,64]{5,4,3,2,1,0:T(8,128)(2,1)} %bitcast.9, f32[64,128]{1,0:T(8,128)} %constant.6.clone.trig_hbm, ...), custom_call_target="tpu_custom_call" | custom-call | tf_op jit(solution)/shard_map/pallas_call | solution.py:463
  46.5 1.9 %copy.9 = bf16[64,4,512]{2,1,0:T(4,128)(2,1)} copy(bf16[64,4,512]{2,0,1:T(8,128)(2,1)} %bitcast.7) | data formatting | bytes 524288 | tf_op jit(solution)/shard_map/transpose | solution.py:502
